TPU v7x, 32 devices: a whole 2x2x4 slice. The times are simulated.
32 devices in a mesh: groups: 2 (over x), goal: 16 (over z, y, core).
Axes of the slice: x: 2, y: 2, z: 4, core: 2. Of those that a mesh axis runs over, the one named last changes fastest.
Arguments:
- queries: bfloat16 [128, 64, 4096], P(('groups', 'goal')), parts along dimension 0, may hold values from -8 to 8
- goal_keys: bfloat16 [32, 256, 4096], P(('groups', 'goal')), parts along dimension 0, may hold values from -8 to 8
- goal_values: bfloat16 [32, 256, 4096], P(('groups', 'goal')), parts along dimension 0, may hold values from -6 to 6
- out_weight: bfloat16 [4096, 2048], P('goal'), may hold values from -0.5 to 0.5
- tactic_goal: int32 [128, 1], P(('groups', 'goal')), parts along dimension 0, may hold values from 0 to 15
- tactic_len: int32 [128], P(('groups', 'goal')), parts along dimension 0, may hold values from 1 to 64
Outputs:
- projected: bfloat16 [128, 64, 2048], P(('groups', 'goal')), parts along dimension 0
There are 2 independent parts, one for each index of `groups`. A program takes and returns all parts, laid end to end along the dimension named above; an argument that names none is the same for every part. Nothing has to cross between parts.
Inputs may be any that keep to these rules, and one draw needn't show every extreme that they name: `tactic_goal`: every goal is read by at least one tactic; tactics per goal are uneven. `tactic_len`: the live positions of a tactic are its leading ones.
All inputs are finite; a program needn't handle non-finite values.
Results may differ from a plain program's by a relative error of at most 0.01.
Values may be sent and summed in bfloat16 or wider, within the bound.
A program may use at most 192 MiB of HBM per device.

v0:
```python
import math
import jax
import jax.numpy as jnp
from jax import lax
from jax.sharding import PartitionSpec as P

DH = 64


def attend_block(query_block, keys_heads, values_heads, block_ids):
    tact_count = query_block.shape[0]
    row_count = query_block.shape[1]
    width_local = query_block.shape[2]
    head_count = width_local // DH
    keys_tact = jnp.take(keys_heads, block_ids, axis=0).reshape(tact_count, -1, head_count, DH)
    vals_tact = jnp.take(values_heads, block_ids, axis=0).reshape(tact_count, -1, head_count, DH)
    query_four = query_block.reshape(tact_count, row_count, head_count, DH)
    scores = jnp.einsum(
        "tihd,tjhd->thij", query_four, keys_tact, preferred_element_type=jnp.float32
    )
    biggest = jnp.max(scores, axis=-1, keepdims=True)
    powers = jnp.exp(scores - biggest)
    weights = (powers / jnp.sum(powers, axis=-1, keepdims=True)).astype(jnp.bfloat16)
    attended = jnp.einsum("thij,tjhd->tihd", weights, vals_tact, preferred_element_type=jnp.float32)
    return attended.reshape(tact_count, row_count, width_local).astype(jnp.bfloat16)


def attend(query_piece, keys_heads, values_heads, goal_ids):
    tact_count = query_piece.shape[0]
    row_count = query_piece.shape[1]
    width_local = query_piece.shape[2]
    block_size = math.gcd(tact_count, 64)
    block_count = tact_count // block_size
    query_blocks = query_piece.reshape(block_count, block_size, row_count, width_local)
    id_blocks = goal_ids.reshape(block_count, block_size)

    def one_block(operands):
        return attend_block(operands[0], keys_heads, values_heads, operands[1])

    results = lax.map(one_block, (query_blocks, id_blocks))
    return results.reshape(tact_count, row_count, width_local)


def shards(queries, goal_keys, goal_values, out_weight, tactic_goal, tactic_len):
    goal_ids = lax.all_gather(tactic_goal[:, 0], "goal", axis=0, tiled=True)
    keys_heads, values_heads = (
        lax.all_to_all(goal_keys, "goal", split_axis=2, concat_axis=0, tiled=True),
        lax.all_to_all(goal_values, "goal", split_axis=2, concat_axis=0, tiled=True),
    )
    query_heads = lax.all_to_all(queries, "goal", split_axis=2, concat_axis=0, tiled=True)
    attended = attend(query_heads, keys_heads, values_heads, goal_ids)
    merged = lax.all_to_all(attended, "goal", split_axis=0, concat_axis=2, tiled=True)
    live_rows = jnp.arange(merged.shape[1])[None, :] < tactic_len[:, None]
    context = jnp.where(live_rows[:, :, None], merged, jnp.zeros_like(merged))
    tact_local = context.shape[0]
    row_count = context.shape[1]
    flat = context.reshape(tact_local * row_count, context.shape[2])
    projected = jnp.dot(
        flat,
        lax.all_gather(out_weight, "goal", axis=0, tiled=True),
        preferred_element_type=jnp.float32,
    )
    return projected.astype(jnp.bfloat16).reshape(tact_local, row_count, out_weight.shape[1])


def solution(mesh):
    return jax.shard_map(
        shards,
        mesh=mesh,
        in_specs=(
            P(("groups", "goal"), None, None),
            P(("groups", "goal"), None, None),
            P(("groups", "goal"), None, None),
            P("goal", None),
            P(("groups", "goal"), None),
            P(("groups", "goal")),
        ),
        out_specs=P(("groups", "goal"), None, None),
        check_vma=False,
    )
```

profile of v0, /device:TPU:13, one launch (start us, length us, event | category | flops | bytes accessed | tf_op | source)
XLA Modules:
  0.0 509.1 jit_solution(2314349538631211243)
XLA Ops:
  7.3 10.1 %copy.23 = bf16[1,256,4096]{1,0,2:T(2,128)(2,1)} copy(bf16[1,256,4096]{2,1,0:T(8,128)(2,1)} %param.10) | data formatting | bytes 4194304 | tf_op args[2]
  17.8 21.7 %reduce.1 = bf16[4096,256]{1,0:T(8,128)(2,1)S(1)} reduce(bf16[4096,1,256]{2,1,0:T(2,128)(2,1)} %bitcast.58, bf16[]{:T(256)} %broadcast.32), dimensions={1}, to_apply=%bitcast.44.reduce_sub_computation | reduce | bytes 4194306
  41.6 6.6 %all-to-all-start = ((bf16[16,2,32768]{2,1,0:T(2,128)(2,1)}), bf16[16,2,32768]{2,1,0:T(2,128)(2,1)S(1)}, u32[]{:S(2)}, u32[]{:S(2)}) async-start(bf16[16,2,32768]{2,1,0:T(2,128)(2,1)} %reshape.91), calls=%async_computation | async-start | bytes 4194304 | tf_op jit(solution)/shard_map/all_to_all | solution.py:48
  48.1 10.1 %copy.26 = bf16[1,256,4096]{1,0,2:T(2,128)(2,1)} copy(bf16[1,256,4096]{2,1,0:T(8,128)(2,1)} %param.9) | data formatting | bytes 4194304 | tf_op args[1]
  58.2 23.0 %reduce = bf16[4096,256]{1,0:T(8,128)(2,1)} reduce(bf16[4096,1,256]{2,1,0:T(2,128)(2,1)} %bitcast.59, bf16[]{:T(256)} %broadcast.32), dimensions={1}, to_apply=%bitcast.46.reduce_sub_computation | reduce | bytes 4194306
  85.1 58.2 %all-to-all-done = bf16[16,2,32768]{2,1,0:T(2,128)(2,1)S(1)} async-done(((bf16[16,2,32768]{2,1,0:T(2,128)(2,1)}), bf16[16,2,32768]{2,1,0:T(2,128)(2,1)S(1)}, u32[]{:S(2)}, u32[]{:S(2)}) %all-to-all-start) | async-done | bytes 2097184 | tf_op jit(solution)/shard_map/all_to_all | solution.py:48
  147.7 7.0 %copy.29 = bf16[4,64,4096]{1,0,2:T(4,128)(2,1)} copy(bf16[4,64,4096]{2,1,0:T(8,128)(2,1)} %param.8) | data formatting | bytes 4194304 | tf_op args[0]
  154.7 7.5 %reshape.95 = bf16[16,2,32768]{2,1,0:T(2,128)(2,1)} reshape(bf16[4096,4,64]{2,1,0:T(4,128)(2,1)} %bitcast.63) | data formatting | bytes 4194304
  162.3 52.0 %all-to-all-done.1 = bf16[16,2,32768]{2,1,0:T(2,128)(2,1)} async-done(((bf16[16,2,32768]{2,1,0:T(2,128)(2,1)}), bf16[16,2,32768]{2,1,0:T(2,128)(2,1)}, u32[]{:S(2)}, u32[]{:S(2)}) %all-to-all-start.1) | async-done | bytes 2097184 | tf_op jit(solution)/shard_map/all_to_all | solution.py:47
  220.4 44.1 %all-reduce = s32[64]{0:T(128)S(1)} all-reduce(s32[64]{0:T(128)S(1)} %bitcast_dynamic-update-slice_fusion), channel_id=2, replica_groups=mesh['groups'=2,'goal'=16] {'goal'}, use_global_device_ids=true, to_apply=%add | all-reduce | flops 64 | bytes 512 | tf_op jit(solution)/shard_map/all_gather | solution.py:45
  264.5 6.8 %reshape.92 = bf16[4096,1,256]{2,1,0:T(2,128)(2,1)} reshape(bf16[16,2,32768]{2,1,0:T(2,128)(2,1)S(1)} %all-to-all-done) | data formatting | bytes 4194304
  278.0 10.5 %reshape.94 = bf16[4096,1,256]{2,1,0:T(2,128)(2,1)} reshape(bf16[16,2,32768]{2,1,0:T(2,128)(2,1)} %all-to-all-done.1) | data formatting | bytes 4194304
  296.3 5.5 %gather_fusion = bf16[64,256,256]{2,1,0:T(8,128)(2,1)} fusion(bf16[16,256,256]{2,1,0:T(8,128)(2,1)S(1)} %bitcast.56, s32[1024]{0:T(1024)S(1)} %pad_clamp_fusion), kind=kCustom, calls=%fused_computation.clone | custom fusion | bytes 16777472 | tf_op jit(solution)/shard_map/while/body/eval_jaxpr/jit(_take)/gather | solution.py:16
  301.8 7.1 %gather_fusion.1 = bf16[64,256,256]{2,1,0:T(8,128)(2,1)} fusion(bf16[16,256,256]{2,1,0:T(8,128)(2,1)} %bitcast.57, s32[1024]{0:T(1024)S(1)} %pad_clamp_fusion), kind=kCustom, calls=%fused_computation.1.clone | custom fusion | bytes 16777472 | tf_op jit(solution)/shard_map/while/body/eval_jaxpr/jit(_take)/gather | solution.py:15
  308.9 11.6 %broadcast_select_fusion = (bf16[64,256,256]{2,1,0:T(8,128)(2,1)}, bf16[64,256,256]{2,1,0:T(8,128)(2,1)}) fusion(bf16[64,256,256]{2,1,0:T(8,128)(2,1)} %gather_fusion.1, pred[64]{0:T(512)(128)(4,1)S(1)} %compare_and_fusion, bf16[64,256,256]{2,1,0:T(8,128)(2,1)} %gather_fusion), kind=kLoop, calls=%fused_computation.9 | loop fusion | flops 8388608 | bytes 33554496 | tf_op jit(solution)/shard_map/while/body/eval_jaxpr/jit(_take)/select_n | solution.py:15
  320.5 11.9 %copy.28 = bf16[64,256,256]{1,2,0:T(8,128)(2,1)} copy(bf16[64,256,256]{2,1,0:T(8,128)(2,1)} %get-tuple-element.16) | data formatting | bytes 16777216 | tf_op jit(solution)/shard_map/while/body/eval_jaxpr/jit(_take)/select_n | solution.py:15
  332.4 7.5 %reshape.96 = bf16[4096,4,64]{2,1,0:T(4,128)(2,1)} reshape(bf16[16,2,32768]{2,1,0:T(2,128)(2,1)} %all-to-all-done.2) | data formatting | bytes 4194304
  348.5 11.9 %copy.25 = bf16[64,256,256]{1,2,0:T(8,128)(2,1)} copy(bf16[64,256,256]{2,1,0:T(8,128)(2,1)} %get-tuple-element.17) | data formatting | bytes 16777216 | tf_op jit(solution)/shard_map/while/body/eval_jaxpr/jit(_take)/select_n | solution.py:16
  360.4 12.7 %fusion.6 = f32[64,4,256,64]{2,3,1,0:T(8,128)} fusion(bf16[64,256,4,64]{1,3,2,0:T(8,128)(2,1)} %bitcast.55, bf16[64,64,4,64]{3,2,1,0:T(4,128)(2,1)} %reshape.60), kind=kOutput, calls=%fused_computation.11 | convolution fusion | flops 536870912 | bytes 27262976 | tf_op jit(solution)/shard_map/while/body/eval_jaxpr/tihd,tjhd->thij/dot_general | solution.py:18
  373.1 14.6 %fusion.18 = f32[64,4,64]{2,1,0:T(4,128)S(1)} fusion(f32[64,4,256,64]{2,3,1,0:T(8,128)} %fusion.6), kind=kOutput, calls=%fused_computation.25 | output fusion | flops 8388863 | bytes 16842752 | tf_op jit(solution)/shard_map/while/body/eval_jaxpr/sub | solution.py:22
  387.7 43.3 %fusion.8 = bf16[64,4,64,64]{3,2,1,0:T(8,128)(2,1)} fusion(bf16[64,256,4,64]{1,3,2,0:T(8,128)(2,1)} %bitcast.67, f32[64,4,64]{2,1,0:T(4,128)S(1)} %fusion.18, f32[64,4,256,64]{2,3,1,0:T(8,128)} %fusion.6), kind=kOutput, calls=%fused_computation.13 | convolution fusion | flops 550519040 | bytes 27328512 | tf_op jit(solution)/shard_map/while/body/eval_jaxpr/thij,tjhd->tihd/dot_general | solution.py:24
  435.9 7.5 %all-to-all-start.3 = ((bf16[64,64,256]{2,1,0:T(8,128)(2,1)}), bf16[64,64,256]{2,1,0:T(8,128)(2,1)S(1)}, u32[]{:S(2)}, u32[]{:S(2)}) async-start(bf16[64,64,256]{2,1,0:T(8,128)(2,1)} %copy.32), calls=%async_computation.3 | async-start | bytes 4194304 | tf_op jit(solution)/shard_map/all_to_all | solution.py:52
  443.6 47.3 %all-to-all-done.3 = bf16[64,64,256]{2,1,0:T(8,128)(2,1)S(1)} async-done(((bf16[64,64,256]{2,1,0:T(8,128)(2,1)}), bf16[64,64,256]{2,1,0:T(8,128)(2,1)S(1)}, u32[]{:S(2)}, u32[]{:S(2)}) %all-to-all-start.3) | async-done | bytes 2097184 | tf_op jit(solution)/shard_map/all_to_all | solution.py:52
  493.0 9.3 %convolution_convert_fusion = bf16[256,2048]{1,0:T(8,128)(2,1)} fusion(bf16[4096,2048]{1,0:T(8,128)(2,1)} %all-gather.3.cloned.1.call-done, bf16[256,4096]{1,0:T(8,128)(2,1)S(1)} %bitcast.71, pred[256]{0:T(512)(128)(4,1)S(1)} %lt.30), kind=kOutput, calls=%fused_computation.14 | convolution fusion | flops 4296540160 | bytes 19923200 | tf_op jit(solution)/shard_map/dot_general | solution.py:58
  (32 shorter events, 47.3 us)
Async XLA Ops:
  6.5 486.4 %all-gather.3.cloned.1.call-start = ((), (), s32[]{:S(2)}) async-start(), calls=%async_computation.4 | async-start | bytes 17825792 | tf_op jit(solution)/shard_map/all_gather | solution.py:60
  41.6 101.8 %all-to-all-start = ((bf16[16,2,32768]{2,1,0:T(2,128)(2,1)}), bf16[16,2,32768]{2,1,0:T(2,128)(2,1)S(1)}, u32[]{:S(2)}, u32[]{:S(2)}) async-start(bf16[16,2,32768]{2,1,0:T(2,128)(2,1)} %reshape.91), calls=%async_computation | async-start | bytes 4194304 | tf_op jit(solution)/shard_map/all_to_all | solution.py:48
  143.3 71.0 %all-to-all-start.1 = ((bf16[16,2,32768]{2,1,0:T(2,128)(2,1)}), bf16[16,2,32768]{2,1,0:T(2,128)(2,1)}, u32[]{:S(2)}, u32[]{:S(2)}) async-start(bf16[16,2,32768]{2,1,0:T(2,128)(2,1)} %reshape.93), calls=%async_computation.1 | async-start | bytes 4194304 | tf_op jit(solution)/shard_map/all_to_all | solution.py:47
  147.7 71.4 %copy-start.2 = (u32[32]{0:T(128)S(1)}, u32[32]{0:T(128)}, u32[]{:S(2)}) copy-start(u32[32]{0:T(128)} %constant.37) | copy-start | bytes 388
  147.7 72.6 %copy-start = (s32[4,1]{0,1:T(1,128)S(1)}, s32[4,1]{0,1:T(1,128)}, u32[]{:S(2)}) copy-start(s32[4,1]{0,1:T(1,128)} %param.12) | copy-start | bytes 52
  214.3 118.2 %all-to-all-start.2 = ((bf16[16,2,32768]{2,1,0:T(2,128)(2,1)}), bf16[16,2,32768]{2,1,0:T(2,128)(2,1)}, u32[]{:S(2)}, u32[]{:S(2)}) async-start(bf16[16,2,32768]{2,1,0:T(2,128)(2,1)} %reshape.95), calls=%async_computation.2 | async-start | bytes 4194304 | tf_op jit(solution)/shard_map/all_to_all | solution.py:50
  431.1 12.3 %copy-start.1 = (s32[4]{0:T(128)S(1)}, s32[4]{0:T(128)}, u32[]{:S(2)}) copy-start(s32[4]{0:T(128)} %param.13) | copy-start | bytes 52
  435.9 54.9 %all-to-all-start.3 = ((bf16[64,64,256]{2,1,0:T(8,128)(2,1)}), bf16[64,64,256]{2,1,0:T(8,128)(2,1)S(1)}, u32[]{:S(2)}, u32[]{:S(2)}) async-start(bf16[64,64,256]{2,1,0:T(8,128)(2,1)} %copy.32), calls=%async_computation.3 | async-start | bytes 4194304 | tf_op jit(solution)/shard_map/all_to_all | solution.py:52
Sparse Core Ops, SparseCore 0:
  9.5 193.1 all-gather.2
where the time goes:
time: 512 us; the launch traced here: 509 us
  waiting for transfers between devices  158 us (31%)
  local copies, waits for them, and re-layouts  133 us (26%)
  other arithmetic  70.9 us (14%)
  matrix products  65.3 us (13%)
  blocking collectives  44.1 us (9%)
  starting transfers between devices  23.2 us (5%)
  between operations  14.2 us (3%)
    unnamed x22, local copies, waits for them, and re-layouts  75.4 us
    all_to_all x1, waiting for transfers between devices, shards(): lax.all_to_all(goal_values, 'goal', split_axis=2, concat_axis=0, tiled=True)  58.2 us
    all_to_all x1, waiting for transfers between devices, shards(): lax.all_to_all(goal_keys, 'goal', split_axis=2, concat_axis=0, tiled=True)  52 us
    all_to_all x1, waiting for transfers between devices, shards(): lax.all_to_all(attended, 'goal', split_axis=0, concat_axis=2, tiled=True)  47.3 us
    unnamed x2, other arithmetic  44.6 us
    all_gather x1, blocking collectives, shards(): goal_ids = lax.all_gather(tactic_goal[:, 0], 'goal', axis=0, tiled=True)  44.1 us
    dot_general x1, matrix products, attend_block(): jnp.einsum('thij,tjhd->tihd', weights, vals_tact, preferred_element_type=...  43.3 us
    sub x1, other arithmetic, attend_block(): powers = jnp.exp(scores - biggest)  14.6 us
  transfers between devices with their start and end apart: 5, of which 3 were waited for; matrix products, arithmetic and copies ran while one was open for 51% of the time, Pallas kernels for 0%

commit v1 on v0

--- a/solution.py
+++ b/solution.py
@@ -5,6 +5,29 @@
 from jax.sharding import PartitionSpec as P
 
 DH = 64
+
+
+def in_blocks(shard, dim, size):
+    shape = shard.shape
+    parts = shard.reshape(*shape[:dim], size, shape[dim] // size, *shape[dim + 1 :])
+    return jnp.moveaxis(parts, dim, 0)
+
+
+def laid_out(blocks, dim):
+    blocks = jnp.moveaxis(blocks, 0, dim)
+    lengths = blocks.shape
+    return blocks.reshape(*lengths[:dim], lengths[dim] * lengths[dim + 1], *lengths[dim + 2 :])
+
+
+def exchange_in_pairs(x, axis, split_dim, concat_dim):
+    size, position = (lax.axis_size(axis), lax.axis_index(axis))
+    blocks = in_blocks(x, split_dim, size)
+    done = [blocks[position]]
+    for step in range(1, size):
+        sent = blocks[position ^ step]
+        done.append(lax.ppermute(sent, axis, [(i, i ^ step) for i in range(size)]))
+    blocks = jnp.stack(done)[position ^ jnp.arange(size)]
+    return laid_out(blocks, concat_dim)
 
 
 def attend_block(query_block, keys_heads, values_heads, block_ids):
@@ -45,7 +68,7 @@
     goal_ids = lax.all_gather(tactic_goal[:, 0], "goal", axis=0, tiled=True)
     keys_heads, values_heads = (
         lax.all_to_all(goal_keys, "goal", split_axis=2, concat_axis=0, tiled=True),
-        lax.all_to_all(goal_values, "goal", split_axis=2, concat_axis=0, tiled=True),
+        exchange_in_pairs(goal_values, "goal", 2, 0),
     )
     query_heads = lax.all_to_all(queries, "goal", split_axis=2, concat_axis=0, tiled=True)
     attended = attend(query_heads, keys_heads, values_heads, goal_ids)

time: 512 us -> 490 us (0.957)
  waiting for transfers between devices: 158 us -> 103 us
  starting transfers between devices: 23.2 us -> 49.9 us
  other arithmetic: 70.9 us -> 48.1 us
  blocking collectives: 44.1 us -> 64.4 us
  local copies, waits for them, and re-layouts: 133 us -> 143 us
    all_to_all x1 -> x0, waiting for transfers between devices: 58.2 us -> none  [shards(): lax.all_to_all(goal_values, 'goal', split_axis=2, concat_axis=0, tiled=True)]
    ppermute x0 -> x15, waiting for transfers between devices: none -> 55.3 us  [exchange_in_pairs(): done.append(lax.ppermute(sent, axis, [(i, i ^ step) for i in range(size)]))]
    all_to_all x1, waiting for transfers between devices: 52 us -> 0.01 us  [shards(): lax.all_to_all(goal_keys, 'goal', split_axis=2, concat_axis=0, tiled=True)]
    ppermute x0 -> x15, starting transfers between devices: none -> 32.7 us  [exchange_in_pairs(): done.append(lax.ppermute(sent, axis, [(i, i ^ step) for i in range(size)]))]
    unnamed x2 -> x1, other arithmetic: 44.6 us -> 21.7 us
    all_gather x1, blocking collectives: 44.1 us -> 64.4 us  [shards(): goal_ids = lax.all_gather(tactic_goal[:, 0], 'goal', axis=0, tiled=True)]
    another operation x0 -> x18, local copies, waits for them, and re-layouts: none -> 13.2 us
    all_to_all x1 -> x0, starting transfers between devices: 6.55 us -> none  [shards(): lax.all_to_all(goal_values, 'goal', split_axis=2, concat_axis=0, tiled=True)]
  transfers between devices with their start and end apart: 5 -> 19, of which waited for: 3 -> 5; matrix products, arithmetic and copies ran while one was open for 51% -> 50% of each run, Pallas kernels for 0% -> 0%
where the time goes in v1:
time: 490 us; the launch traced here: 488 us
  local copies, waits for them, and re-layouts  143 us (29%)
  waiting for transfers between devices  103 us (21%)
  matrix products  65.2 us (13%)
  blocking collectives  64.4 us (13%)
  starting transfers between devices  49.9 us (10%)
  other arithmetic  48.1 us (10%)
  between operations  14.2 us (3%)
    unnamed x36, local copies, waits for them, and re-layouts  74.8 us
    all_gather x1, blocking collectives, shards(): goal_ids = lax.all_gather(tactic_goal[:, 0], 'goal', axis=0, tiled=True)  64.4 us
    ppermute x15, waiting for transfers between devices, exchange_in_pairs(): done.append(lax.ppermute(sent, axis, [(i, i ^ step) for i in range(size)]))  55.3 us
    all_to_all x1, waiting for transfers between devices, shards(): lax.all_to_all(attended, 'goal', split_axis=0, concat_axis=2, tiled=True)  47.3 us
    dot_general x1, matrix products, attend_block(): jnp.einsum('thij,tjhd->tihd', weights, vals_tact, preferred_element_type=...  43.2 us
    ppermute x15, starting transfers between devices, exchange_in_pairs(): done.append(lax.ppermute(sent, axis, [(i, i ^ step) for i in range(size)]))  32.7 us
    unnamed x1, other arithmetic  21.7 us
    sub x1, other arithmetic, attend_block(): powers = jnp.exp(scores - biggest)  14.7 us
  transfers between devices with their start and end apart: 19, of which 5 were waited for; matrix products, arithmetic and copies ran while one was open for 50% of the time, Pallas kernels for 0%

profile of v1, /device:TPU:13, one launch (start us, length us, event | category | flops | bytes accessed | tf_op | source)
XLA Modules:
  0.0 487.7 jit_solution(9988115716624123245)
XLA Ops:
  7.3 10.0 %copy.55 = bf16[1,256,4096]{1,0,2:T(2,128)(2,1)} copy(bf16[1,256,4096]{2,1,0:T(8,128)(2,1)} %param.9) | data formatting | bytes 4194304 | tf_op args[1]
  17.8 21.7 %reduce = bf16[4096,256]{1,0:T(8,128)(2,1)S(1)} reduce(bf16[4096,1,256]{2,1,0:T(2,128)(2,1)} %bitcast.102, bf16[]{:T(256)} %broadcast.67), dimensions={1}, to_apply=%bitcast.91.reduce_sub_computation | reduce | bytes 4194306
  41.5 6.6 %all-to-all-start = ((bf16[16,2,32768]{2,1,0:T(2,128)(2,1)}), bf16[16,2,32768]{2,1,0:T(2,128)(2,1)S(1)}, u32[]{:S(2)}, u32[]{:S(2)}) async-start(bf16[16,2,32768]{2,1,0:T(2,128)(2,1)} %reshape.157), calls=%async_computation | async-start | bytes 4194304 | tf_op jit(solution)/shard_map/all_to_all | solution.py:70
  68.9 64.4 %all-reduce = s32[64]{0:T(128)S(1)} all-reduce(s32[64]{0:T(128)S(1)} %bitcast_dynamic-update-slice_fusion.16), channel_id=2, replica_groups=mesh['groups'=2,'goal'=16] {'goal'}, use_global_device_ids=true, to_apply=%add | all-reduce | flops 64 | bytes 512 | tf_op jit(solution)/shard_map/all_gather | solution.py:68
  136.0 6.9 %copy.58 = bf16[4,64,4096]{1,0,2:T(4,128)(2,1)} copy(bf16[4,64,4096]{2,1,0:T(8,128)(2,1)} %param.8) | data formatting | bytes 4194304 | tf_op args[0]
  142.9 7.5 %reshape.159 = bf16[16,2,32768]{2,1,0:T(2,128)(2,1)} reshape(bf16[4096,4,64]{2,1,0:T(4,128)(2,1)} %bitcast.105) | data formatting | bytes 4194304
  150.5 8.5 %collective-permute-start.5 = (bf16[1,256,256]{2,1,0:T(8,128)(2,1)S(1)}, bf16[1,256,256]{2,1,0:T(8,128)(2,1)S(1)}, u32[]{:S(2)}, u32[]{:S(2)}) collective-permute-start(bf16[1,256,256]{2,1,0:T(8,128)(2,1)S(1)} %bitcast.129), channel_id=1, source_target_pairs={{0,6},{1,7},{2,4},{3,5},{4,2},{5,3},{6,0},{7,1},{8,14},{9,15},{10,... | collective-permute-start | bytes 393224 | tf_op jit(solution)/shard_map/ppermute | solution.py:28
  175.0 6.1 %all-to-all-start.1 = ((bf16[16,2,32768]{2,1,0:T(2,128)(2,1)}), bf16[16,2,32768]{2,1,0:T(2,128)(2,1)}, u32[]{:S(2)}, u32[]{:S(2)}) async-start(bf16[16,2,32768]{2,1,0:T(2,128)(2,1)} %reshape.159), calls=%async_computation.1 | async-start | bytes 4194304 | tf_op jit(solution)/shard_map/all_to_all | solution.py:73
  186.9 10.0 %collective-permute-start.13 = (bf16[1,256,256]{2,1,0:T(8,128)(2,1)S(1)}, bf16[1,256,256]{2,1,0:T(8,128)(2,1)S(1)}, u32[]{:S(2)}, u32[]{:S(2)}) collective-permute-start(bf16[1,256,256]{2,1,0:T(8,128)(2,1)S(1)} %bitcast.116), channel_id=1, source_target_pairs={{0,14},{1,15},{2,12},{3,13},{4,10},{5,11},{6,8},{7,9},{8,6},{9,7},... | collective-permute-start | bytes 393224 | tf_op jit(solution)/shard_map/ppermute | solution.py:28
  202.2 48.8 %collective-permute-done.11 = bf16[1,256,256]{2,1,0:T(8,128)(2,1)S(1)} collective-permute-done((bf16[1,256,256]{2,1,0:T(8,128)(2,1)S(1)}, bf16[1,256,256]{2,1,0:T(8,128)(2,1)S(1)}, u32[]{:S(2)}, u32[]{:S(2)}) %collective-permute-start.11) | collective-permute-done | bytes 131104 | tf_op jit(solution)/shard_map/ppermute | solution.py:28
  262.3 5.5 %gather_fusion.1 = bf16[64,256,256]{2,1,0:T(8,128)(2,1)} fusion(bf16[16,256,256]{2,1,0:T(8,128)(2,1)S(1)} %gather_fusion, s32[1024]{0:T(1024)S(1)} %pad_clamp_fusion), kind=kCustom, calls=%fused_computation.clone | custom fusion | bytes 16777472 | tf_op jit(solution)/shard_map/while/body/eval_jaxpr/jit(_take)/gather | solution.py:39
  267.9 10.5 %reshape.158 = bf16[4096,1,256]{2,1,0:T(2,128)(2,1)} reshape(bf16[16,2,32768]{2,1,0:T(2,128)(2,1)} %copy-done) | data formatting | bytes 4194304
  285.1 5.5 %gather_fusion.2 = bf16[64,256,256]{2,1,0:T(8,128)(2,1)} fusion(bf16[16,256,256]{2,1,0:T(8,128)(2,1)S(1)} %bitcast.101, s32[1024]{0:T(1024)S(1)} %pad_clamp_fusion), kind=kCustom, calls=%fused_computation.1.clone | custom fusion | bytes 16777472 | tf_op jit(solution)/shard_map/while/body/eval_jaxpr/jit(_take)/gather | solution.py:38
  290.6 11.6 %broadcast_select_fusion = (bf16[64,256,256]{2,1,0:T(8,128)(2,1)}, bf16[64,256,256]{2,1,0:T(8,128)(2,1)}) fusion(bf16[64,256,256]{2,1,0:T(8,128)(2,1)} %gather_fusion.2, pred[64]{0:T(512)(128)(4,1)S(1)} %compare_and_fusion, bf16[64,256,256]{2,1,0:T(8,128)(2,1)} %gather_fusion.1), kind=kLoop, calls=%fused_computation.10 | loop fusion | flops 8388608 | bytes 33554496 | tf_op jit(solution)/shard_map/while/body/eval_jaxpr/jit(_take)/select_n | solution.py:38
  302.2 11.9 %copy.57 = bf16[64,256,256]{1,2,0:T(8,128)(2,1)} copy(bf16[64,256,256]{2,1,0:T(8,128)(2,1)} %get-tuple-element.40) | data formatting | bytes 16777216 | tf_op jit(solution)/shard_map/while/body/eval_jaxpr/jit(_take)/select_n | solution.py:38
  314.1 7.4 %reshape.160 = bf16[4096,4,64]{2,1,0:T(4,128)(2,1)} reshape(bf16[16,2,32768]{2,1,0:T(2,128)(2,1)} %all-to-all-done.1) | data formatting | bytes 4194304
  321.6 5.4 %copy.59 = bf16[4,64,16,256]{3,1,0,2:T(8,128)(2,1)S(1)} copy(bf16[4,64,16,256]{1,0,3,2:T(4,128)(2,1)} %bitcast.104) | data formatting | bytes 4194304 | tf_op jit(solution)/shard_map/all_to_all | solution.py:73
  330.2 11.9 %copy.54 = bf16[64,256,256]{1,2,0:T(8,128)(2,1)} copy(bf16[64,256,256]{2,1,0:T(8,128)(2,1)} %get-tuple-element.41) | data formatting | bytes 16777216 | tf_op jit(solution)/shard_map/while/body/eval_jaxpr/jit(_take)/select_n | solution.py:39
  342.1 12.7 %fusion.6 = f32[64,4,256,64]{2,3,1,0:T(8,128)} fusion(bf16[64,256,4,64]{1,3,2,0:T(8,128)(2,1)} %bitcast.100, bf16[64,64,4,64]{3,2,1,0:T(4,128)(2,1)} %reshape.115), kind=kOutput, calls=%fused_computation.12 | convolution fusion | flops 536870912 | bytes 27262976 | tf_op jit(solution)/shard_map/while/body/eval_jaxpr/tihd,tjhd->thij/dot_general | solution.py:41
  354.8 14.7 %fusion.19 = f32[64,4,64]{2,1,0:T(4,128)S(1)} fusion(f32[64,4,256,64]{2,3,1,0:T(8,128)} %fusion.6), kind=kOutput, calls=%fused_computation.61 | output fusion | flops 8388863 | bytes 16842752 | tf_op jit(solution)/shard_map/while/body/eval_jaxpr/sub | solution.py:45
  369.5 43.2 %fusion.8 = bf16[64,4,64,64]{3,2,1,0:T(8,128)(2,1)} fusion(bf16[64,256,4,64]{1,3,2,0:T(8,128)(2,1)} %bitcast.108, f32[64,4,64]{2,1,0:T(4,128)S(1)} %fusion.19, f32[64,4,256,64]{2,3,1,0:T(8,128)} %fusion.6), kind=kOutput, calls=%fused_computation.14 | convolution fusion | flops 550519040 | bytes 27328512 | tf_op jit(solution)/shard_map/while/body/eval_jaxpr/thij,tjhd->tihd/dot_general | solution.py:47
  412.7 4.8 copy.61
  422.1 47.3 %all-to-all-done.2 = bf16[64,64,256]{2,1,0:T(8,128)(2,1)S(1)} async-done(((bf16[64,64,256]{2,1,0:T(8,128)(2,1)}), bf16[64,64,256]{2,1,0:T(8,128)(2,1)S(1)}, u32[]{:S(2)}, u32[]{:S(2)}) %all-to-all-start.2) | async-done | bytes 2097184 | tf_op jit(solution)/shard_map/all_to_all | solution.py:75
  471.5 9.3 %convolution_convert_fusion = bf16[256,2048]{1,0:T(8,128)(2,1)} fusion(bf16[4096,2048]{1,0:T(8,128)(2,1)} %all-gather.3.cloned.1.call-done, bf16[256,4096]{1,0:T(8,128)(2,1)S(1)} %bitcast.114, pred[256]{0:T(512)(128)(4,1)S(1)} %lt.88), kind=kOutput, calls=%fused_computation.15 | convolution fusion | flops 4296540160 | bytes 19923200 | tf_op jit(solution)/shard_map/dot_general | solution.py:81
  (93 shorter events, 81.2 us)
Async XLA Ops:
  6.5 465.0 %all-gather.3.cloned.1.call-start = ((), (), s32[]{:S(2)}) async-start(), calls=%async_computation.3 | async-start | bytes 17825792 | tf_op jit(solution)/shard_map/all_gather | solution.py:83
  41.5 132.2 %all-to-all-start = ((bf16[16,2,32768]{2,1,0:T(2,128)(2,1)}), bf16[16,2,32768]{2,1,0:T(2,128)(2,1)S(1)}, u32[]{:S(2)}, u32[]{:S(2)}) async-start(bf16[16,2,32768]{2,1,0:T(2,128)(2,1)} %reshape.157), calls=%async_computation | async-start | bytes 4194304 | tf_op jit(solution)/shard_map/all_to_all | solution.py:70
  52.1 15.4 %copy-start.3 = (u32[32]{0:T(128)S(1)}, u32[32]{0:T(128)}, u32[]{:S(2)}) copy-start(u32[32]{0:T(128)} %constant.76) | copy-start | bytes 388
  52.1 16.7 %copy-start.1 = (s32[4,1]{0,1:T(1,128)S(1)}, s32[4,1]{0,1:T(1,128)}, u32[]{:S(2)}) copy-start(s32[4,1]{0,1:T(1,128)} %param.12) | copy-start | bytes 52
  56.3 94.2 %collective-permute-start = (bf16[1,256,256]{2,1,0:T(8,128)(2,1)}, bf16[1,256,256]{2,1,0:T(8,128)(2,1)}, u32[]{:S(2)}, u32[]{:S(2)}) collective-permute-start(bf16[1,256,256]{2,1,0:T(8,128)(2,1)} %bitcast.128), channel_id=1, source_target_pairs={{0,1},{1,0},{2,3},{3,2},{4,5},{5,4},{6,7},{7,6},{8,9},{9,8},{10,11... | collective-permute-start | bytes 393224 | tf_op jit(solution)/shard_map/ppermute | solution.py:28
  58.3 102.2 %collective-permute-start.1 = (bf16[1,256,256]{2,1,0:T(8,128)(2,1)}, bf16[1,256,256]{2,1,0:T(8,128)(2,1)}, u32[]{:S(2)}, u32[]{:S(2)}) collective-permute-start(bf16[1,256,256]{2,1,0:T(8,128)(2,1)} %bitcast.127), channel_id=1, source_target_pairs={{0,2},{1,3},{2,0},{3,1},{4,6},{5,7},{6,4},{7,5},{8,10},{9,11},{10,... | collective-permute-start | bytes 393224 | tf_op jit(solution)/shard_map/ppermute | solution.py:28
  60.3 102.5 %collective-permute-start.2 = (bf16[1,256,256]{2,1,0:T(8,128)(2,1)}, bf16[1,256,256]{2,1,0:T(8,128)(2,1)}, u32[]{:S(2)}, u32[]{:S(2)}) collective-permute-start(bf16[1,256,256]{2,1,0:T(8,128)(2,1)} %bitcast.126), channel_id=1, source_target_pairs={{0,3},{1,2},{2,1},{3,0},{4,7},{5,6},{6,5},{7,4},{8,11},{9,10},{10,... | collective-permute-start | bytes 393224 | tf_op jit(solution)/shard_map/ppermute | solution.py:28
  63.4 101.0 %collective-permute-start.3 = (bf16[1,256,256]{2,1,0:T(8,128)(2,1)}, bf16[1,256,256]{2,1,0:T(8,128)(2,1)}, u32[]{:S(2)}, u32[]{:S(2)}) collective-permute-start(bf16[1,256,256]{2,1,0:T(8,128)(2,1)} %bitcast.124), channel_id=1, source_target_pairs={{0,4},{1,5},{2,6},{3,7},{4,0},{5,1},{6,2},{7,3},{8,12},{9,13},{10,... | collective-permute-start | bytes 393224 | tf_op jit(solution)/shard_map/ppermute | solution.py:28
  65.4 103.5 %collective-permute-start.4 = (bf16[1,256,256]{2,1,0:T(8,128)(2,1)}, bf16[1,256,256]{2,1,0:T(8,128)(2,1)}, u32[]{:S(2)}, u32[]{:S(2)}) collective-permute-start(bf16[1,256,256]{2,1,0:T(8,128)(2,1)} %bitcast.123), channel_id=1, source_target_pairs={{0,5},{1,4},{2,7},{3,6},{4,1},{5,0},{6,3},{7,2},{8,13},{9,12},{10,... | collective-permute-start | bytes 393224 | tf_op jit(solution)/shard_map/ppermute | solution.py:28
  150.5 20.6 %collective-permute-start.5 = (bf16[1,256,256]{2,1,0:T(8,128)(2,1)S(1)}, bf16[1,256,256]{2,1,0:T(8,128)(2,1)S(1)}, u32[]{:S(2)}, u32[]{:S(2)}) collective-permute-start(bf16[1,256,256]{2,1,0:T(8,128)(2,1)S(1)} %bitcast.129), channel_id=1, source_target_pairs={{0,6},{1,7},{2,4},{3,5},{4,2},{5,3},{6,0},{7,1},{8,14},{9,15},{10,... | collective-permute-start | bytes 393224 | tf_op jit(solution)/shard_map/ppermute | solution.py:28
  160.5 21.3 %collective-permute-start.6 = (bf16[1,256,256]{2,1,0:T(8,128)(2,1)S(1)}, bf16[1,256,256]{2,1,0:T(8,128)(2,1)}, u32[]{:S(2)}, u32[]{:S(2)}) collective-permute-start(bf16[1,256,256]{2,1,0:T(8,128)(2,1)S(1)} %bitcast.125), channel_id=1, source_target_pairs={{0,7},{1,6},{2,5},{3,4},{4,3},{5,2},{6,1},{7,0},{8,15},{9,14},{10,... | collective-permute-start | bytes 393224 | tf_op jit(solution)/shard_map/ppermute | solution.py:28
  162.8 21.8 %collective-permute-start.7 = (bf16[1,256,256]{2,1,0:T(8,128)(2,1)S(1)}, bf16[1,256,256]{2,1,0:T(8,128)(2,1)}, u32[]{:S(2)}, u32[]{:S(2)}) collective-permute-start(bf16[1,256,256]{2,1,0:T(8,128)(2,1)S(1)} %bitcast.122), channel_id=1, source_target_pairs={{0,8},{1,9},{2,10},{3,11},{4,12},{5,13},{6,14},{7,15},{8,0},{9,1},... | collective-permute-start | bytes 393224 | tf_op jit(solution)/shard_map/ppermute | solution.py:28
  164.4 22.5 %collective-permute-start.8 = (bf16[1,256,256]{2,1,0:T(8,128)(2,1)S(1)}, bf16[1,256,256]{2,1,0:T(8,128)(2,1)}, u32[]{:S(2)}, u32[]{:S(2)}) collective-permute-start(bf16[1,256,256]{2,1,0:T(8,128)(2,1)S(1)} %bitcast.121), channel_id=1, source_target_pairs={{0,9},{1,8},{2,11},{3,10},{4,13},{5,12},{6,15},{7,14},{8,1},{9,0},... | collective-permute-start | bytes 393224 | tf_op jit(solution)/shard_map/ppermute | solution.py:28
  168.9 29.7 %collective-permute-start.9 = (bf16[1,256,256]{2,1,0:T(8,128)(2,1)S(1)}, bf16[1,256,256]{2,1,0:T(8,128)(2,1)}, u32[]{:S(2)}, u32[]{:S(2)}) collective-permute-start(bf16[1,256,256]{2,1,0:T(8,128)(2,1)S(1)} %bitcast.120), channel_id=1, source_target_pairs={{0,10},{1,11},{2,8},{3,9},{4,14},{5,15},{6,12},{7,13},{8,2},{9,3},... | collective-permute-start | bytes 393224 | tf_op jit(solution)/shard_map/ppermute | solution.py:28
  171.0 30.5 %collective-permute-start.10 = (bf16[1,256,256]{2,1,0:T(8,128)(2,1)S(1)}, bf16[1,256,256]{2,1,0:T(8,128)(2,1)S(1)}, u32[]{:S(2)}, u32[]{:S(2)}) collective-permute-start(bf16[1,256,256]{2,1,0:T(8,128)(2,1)S(1)} %bitcast.119), channel_id=1, source_target_pairs={{0,11},{1,10},{2,9},{3,8},{4,15},{5,14},{6,13},{7,12},{8,3},{9,2},... | collective-permute-start | bytes 393224 | tf_op jit(solution)/shard_map/ppermute | solution.py:28
  173.7 1.3 copy-start
  175.0 139.1 %all-to-all-start.1 = ((bf16[16,2,32768]{2,1,0:T(2,128)(2,1)}), bf16[16,2,32768]{2,1,0:T(2,128)(2,1)}, u32[]{:S(2)}, u32[]{:S(2)}) async-start(bf16[16,2,32768]{2,1,0:T(2,128)(2,1)} %reshape.159), calls=%async_computation.1 | async-start | bytes 4194304 | tf_op jit(solution)/shard_map/all_to_all | solution.py:73
  181.8 69.2 %collective-permute-start.11 = (bf16[1,256,256]{2,1,0:T(8,128)(2,1)S(1)}, bf16[1,256,256]{2,1,0:T(8,128)(2,1)S(1)}, u32[]{:S(2)}, u32[]{:S(2)}) collective-permute-start(bf16[1,256,256]{2,1,0:T(8,128)(2,1)S(1)} %bitcast.118), channel_id=1, source_target_pairs={{0,12},{1,13},{2,14},{3,15},{4,8},{5,9},{6,10},{7,11},{8,4},{9,5},... | collective-permute-start | bytes 393224 | tf_op jit(solution)/shard_map/ppermute | solution.py:28
  184.6 69.2 %collective-permute-start.12 = (bf16[1,256,256]{2,1,0:T(8,128)(2,1)S(1)}, bf16[1,256,256]{2,1,0:T(8,128)(2,1)S(1)}, u32[]{:S(2)}, u32[]{:S(2)}) collective-permute-start(bf16[1,256,256]{2,1,0:T(8,128)(2,1)S(1)} %bitcast.117), channel_id=1, source_target_pairs={{0,13},{1,12},{2,15},{3,14},{4,9},{5,8},{6,11},{7,10},{8,5},{9,4},... | collective-permute-start | bytes 393224 | tf_op jit(solution)/shard_map/ppermute | solution.py:28
  186.9 69.7 %collective-permute-start.13 = (bf16[1,256,256]{2,1,0:T(8,128)(2,1)S(1)}, bf16[1,256,256]{2,1,0:T(8,128)(2,1)S(1)}, u32[]{:S(2)}, u32[]{:S(2)}) collective-permute-start(bf16[1,256,256]{2,1,0:T(8,128)(2,1)S(1)} %bitcast.116), channel_id=1, source_target_pairs={{0,14},{1,15},{2,12},{3,13},{4,10},{5,11},{6,8},{7,9},{8,6},{9,7},... | collective-permute-start | bytes 393224 | tf_op jit(solution)/shard_map/ppermute | solution.py:28
  198.5 60.9 %collective-permute-start.14 = (bf16[1,256,256]{2,1,0:T(8,128)(2,1)S(1)}, bf16[1,256,256]{2,1,0:T(8,128)(2,1)S(1)}, u32[]{:S(2)}, u32[]{:S(2)}) collective-permute-start(bf16[1,256,256]{2,1,0:T(8,128)(2,1)S(1)} %bitcast.115), channel_id=1, source_target_pairs={{0,15},{1,14},{2,13},{3,12},{4,11},{5,10},{6,9},{7,8},{8,7},{9,6},... | collective-permute-start | bytes 393224 | tf_op jit(solution)/shard_map/ppermute | solution.py:28
  417.5 4.4 copy-start.2
  417.5 51.9 %all-to-all-start.2 = ((bf16[64,64,256]{2,1,0:T(8,128)(2,1)}), bf16[64,64,256]{2,1,0:T(8,128)(2,1)S(1)}, u32[]{:S(2)}, u32[]{:S(2)}) async-start(bf16[64,64,256]{2,1,0:T(8,128)(2,1)} %copy.61), calls=%async_computation.2 | async-start | bytes 4194304 | tf_op jit(solution)/shard_map/all_to_all | solution.py:75
Sparse Core Ops, SparseCore 0:
  9.5 173.0 all-gather.2
